TPU v7x, 128 devices: a whole 4x4x4 slice. The times are simulated.
128 devices in a mesh: row: 16 (over y, x), col: 8 (over z, core).
Axes of the slice: x: 4, y: 4, z: 4, core: 2. Of those that a mesh axis runs over, the one named last changes fastest.
Arguments:
- band_tiles: bfloat16 [16, 128, 256, 256], P('row', 'col'), may hold values from 0.0009994507 to 1
- band_cell: int32 [16, 128], P('row', 'col'), may hold values from 0 to 31, as said below
- band_count: int32 [16, 8], P('row', 'col'), may hold values from 1 to 16, as said below
- matrix_tiles: bfloat16 [16, 64, 256, 256], P('row', 'col'), may hold values from 7.390976e-05 to 0.07421875
- matrix_col: int32 [16, 64], P('row', 'col'), may hold values from 0 to 15
- matrix_live: int32 [16, 64], P('row', 'col'), may hold values 0 or 1
Outputs:
- reached: bfloat16 [8192, 32768], P('row', 'col')
- gained: float32 [], replicated
Inputs may be any that keep to these rules, and one draw needn't show every extreme that they name: The band_cell values of one device's 16 slots are distinct. `band_count`: among the 8 devices of one index of row, the live slots with slot number 16 // 2 or more number at most 8 in all.
All inputs are finite; a program needn't handle non-finite values. No bound on the sum of `matrix_live` on one device may be relied on, other than what follows from the above.
Results may differ from a plain program's by a relative error of at most 0.001.
Values may be sent and summed in bfloat16 or wider, within the bound.
A program may use at most 128 MiB of HBM per device.

v0:
```python
import jax
import jax.numpy as jnp
from jax import lax
from jax.sharding import Mesh
from jax.sharding import PartitionSpec as P

TILES = 128
BR = 2
COL = ("col_0", "col_1")
ROW = ("row_0", "row_1")
ROW_COL = ("row_0", "row_1", "col_0", "col_1")


def rows_for(lines, length):
    spare = -lines.shape[0] % length
    if not spare:
        return lines
    return jnp.concatenate([lines, jnp.zeros((spare, *lines.shape[1:]), lines.dtype)])


def sum_by_parts(shard, axis):
    lines = shard.reshape(-1, *shard.shape[1:][-1:])
    own = lax.psum_scatter(
        rows_for(lines, lax.axis_size(axis)), axis, scatter_dimension=0, tiled=True
    )
    whole = lax.all_gather(own, axis).reshape(-1, *lines.shape[1:])
    return lax.slice_in_dim(whole, 0, len(lines)).reshape(shard.shape)


def over_axes(shard, axes):
    for axis in axes:
        shard = lax.psum(shard, axis)
    return shard


def on_device(band_tiles, band_cell, band_count, matrix_tiles, matrix_col, matrix_live):
    slots_own = band_tiles.shape[1]
    tile = band_tiles.shape[-1]
    n_col = lax.axis_size(COL)
    tcols = TILES // n_col
    places = BR * tcols
    spots = jnp.arange(places, dtype=jnp.int32)
    b_tiles, b_index, b_live = (
        lax.all_gather(matrix_tiles, ROW, axis=0, tiled=True),
        lax.all_gather(matrix_col, ROW, axis=0, tiled=True),
        lax.all_gather(matrix_live, ROW, axis=0, tiled=True),
    )
    flat_tiles = b_tiles.reshape(-1, tile, tile)
    half = slots_own // 2
    front_tiles, a_cell, a_count = (
        lax.all_gather(band_tiles[:, :half], COL, axis=1, tiled=True),
        lax.all_gather(band_cell, COL, axis=1, tiled=True),
        lax.all_gather(band_count, COL, axis=1, tiled=True),
    )
    counts = a_count[0]
    spill = jnp.maximum(counts - half, 0)
    before = jnp.cumsum(spill) - spill
    ending = before + spill
    mine = lax.axis_index(COL)
    own_before = jnp.take(before, mine)
    own_spill = jnp.maximum(band_count[0, 0] - half, 0)
    pack_spot = jnp.arange(half, dtype=jnp.int32)
    upper = jnp.arange(half, dtype=jnp.int32)
    place_w = (
        (pack_spot[:, None] == own_before + upper[None, :]) & (upper[None, :] < own_spill)
    ).astype(jnp.bfloat16)
    packed = jnp.einsum(
        "qs,sxy->qxy", place_w, band_tiles[0, half:], preferred_element_type=jnp.float32
    )
    spilled = (
        sum_by_parts(packed.astype(jnp.bfloat16), COL).astype(jnp.float32).astype(jnp.bfloat16)
    )
    holder = jnp.sum((ending[None, :] <= pack_spot[:, None]).astype(jnp.int32), axis=1)
    holder = jnp.clip(holder, 0, n_col - 1)
    spill_slot = jnp.clip(half + pack_spot - jnp.take(before, holder), 0, slots_own - 1)
    spill_cell = jnp.take(a_cell[0], holder * slots_own + spill_slot)
    spill_valid = pack_spot < jnp.sum(spill)
    front = jnp.arange(n_col * half, dtype=jnp.int32)
    front_source = front // half
    front_slot = front % half
    front_cell = jnp.take(a_cell[0], front_source * slots_own + front_slot)
    front_valid = front_slot < jnp.take(counts, front_source)
    sources = jnp.concatenate([front_source, holder])
    cells = jnp.concatenate([front_cell, spill_cell])
    valid = jnp.concatenate([front_valid, spill_valid])
    tiles = jnp.concatenate([front_tiles[0], spilled], axis=0)
    k_glob = sources * tcols + cells % tcols
    i_loc = cells // tcols
    picked = jnp.take(flat_tiles, k_glob, axis=0)
    picked_index = jnp.take(b_index.reshape(-1), k_glob)
    picked_live = jnp.take(b_live.reshape(-1), k_glob)
    live = (picked_live > 0) & valid
    position = i_loc * tcols + picked_index
    product = jnp.einsum("axy,ayz->axz", tiles, picked, preferred_element_type=jnp.float32)
    weights = ((position[:, None] == spots[None, :]) & live[:, None]).astype(jnp.float32)
    summed = jnp.einsum("ap,axz->pxz", weights, product, precision=lax.Precision.HIGHEST)
    own_live = jnp.arange(slots_own, dtype=jnp.int32) < band_count[0, 0]
    own_w = ((band_cell[0][:, None] == spots[None, :]) & own_live[:, None]).astype(jnp.bfloat16)
    base = jnp.einsum("sp,sxz->pxz", own_w, band_tiles[0], preferred_element_type=jnp.float32)
    expanded = jnp.minimum(1.0, base + summed)
    block = (
        expanded.reshape(BR, tcols, tile, tile)
        .transpose(0, 2, 1, 3)
        .reshape(BR * tile, tcols * tile)
    )
    total = over_axes(jnp.sum(expanded - base), ROW_COL)
    devices = lax.axis_size(ROW) * n_col
    gained = total / (tile * tile * devices * places)
    return (block.astype(jnp.bfloat16), gained)


def solution(mesh):
    split = Mesh(mesh.devices.reshape(4, 4, 4, 2), ("row_0", "row_1", "col_0", "col_1"))
    placed = (
        P(ROW, COL, None, None),
        P(ROW, COL),
        P(ROW, COL),
        P(ROW, COL, None, None),
        P(ROW, COL),
        P(ROW, COL),
    )
    return jax.shard_map(
        on_device, mesh=split, in_specs=placed, out_specs=(P(ROW, COL), P()), check_vma=False
    )
```

profile of v0, /device:TPU:1, one launch (start us, length us, event | category | flops | bytes accessed | tf_op | source)
XLA Modules:
  0.0 311.7 jit_solution(18201135137651149009)
XLA Ops:
  8.0 0.0 copy-start
  8.0 0.0 copy-start.2
  8.0 0.0 copy-start.3
  8.0 0.0 reduce-scatter.2.cloned.1.call-start
  8.9 1.2 dynamic-slice.3
  10.8 0.7 bitcast_dynamic-update-slice_fusion
  11.5 0.8 bitcast_dynamic-update-slice_fusion.1
  12.2 9.8 %all-reduce.2 = (s32[8]{0:T(128)S(1)}, s32[128]{0:T(128)S(1)}) all-reduce(s32[8]{0:T(128)S(1)} %bitcast_dynamic-update-slice_fusion, s32[128]{0:T(128)S(1)} %bitcast_dynamic-update-slice_fusion.1), channel_id=1, replica_groups=mesh['row_0'=4,'row_1'=4,'col_0'=4,'col_1'=2] {'col_0','col_1'}, use_global_device_ids=true, to_apply=%add.1 | all-reduce | flops 136 | bytes 1088
  22.0 0.6 fusion.42
  22.6 0.2 reduce-window.8
  22.8 0.6 dynamic-slice.2
  24.1 1.3 slice.7
  25.4 0.7 convolution_convert_fusion
  26.1 1.2 copy.24
  27.2 0.0 reduce-scatter.2.cloned.1.call-update
  27.3 0.0 all-gather.9.cloned.1.call-start
  27.3 0.5 all-gather.9.cloned.1.call-update
  27.8 0.0 all-gather.11.cloned.1.call-start
  27.9 29.4 %reduce-scatter.2.cloned.1.call-done = bf16[256,256]{1,0:T(8,128)(2,1)} async-done(((bf16[2048,256]{1,0:T(8,128)(2,1)}), bf16[256,256]{1,0:T(8,128)(2,1)}) %reduce-scatter.2.cloned.1.call-update) | async-done | bytes 131088 | tf_op jit(solution)/shard_map/reduce_scatter | solution.py:23
  57.3 0.0 all-gather.11.cloned.1.call-update
  57.3 0.0 all-gather.7.cloned.1.call-start
  57.4 0.0 copy-done
  57.4 1.0 slice.43
  58.4 0.0 all-gather.7.cloned.1.call-update
  58.4 0.1 convert_reduce_fusion
  58.6 0.6 gather_fusion.1
  59.3 0.6 gather_fusion.2
  59.9 0.8 gather_fusion
  60.7 0.0 copy-done.2
  60.7 17.2 %all-gather.1 = s32[16,1,8]{2,1,0:T(1,128)S(1)} all-gather(s32[1,1,8]{2,1,0:T(1,128)S(1)} %bitcast.102), channel_id=1, replica_groups=mesh['row_0'=4,'row_1'=4,'col_0'=4,'col_1'=2] {'row_0','row_1'}, dimensions={0}, use_global_device_ids=true | all-gather | bytes 544 | tf_op jit(solution)/shard_map/all_gather | solution.py:45
  77.9 0.5 broadcast.1065
  78.4 0.7 reduce.7
  79.1 0.1 reshape.382
  79.2 0.0 copy-done.3
  79.2 17.3 %all-gather.2 = s32[16,1,8]{2,1,0:T(1,128)S(1)} all-gather(s32[1,1,8]{2,1,0:T(1,128)S(1)} %bitcast.103), channel_id=1, replica_groups=mesh['row_0'=4,'row_1'=4,'col_0'=4,'col_1'=2] {'row_0','row_1'}, dimensions={0}, use_global_device_ids=true | all-gather | bytes 544 | tf_op jit(solution)/shard_map/all_gather | solution.py:46
  96.5 0.7 reduce.8
  97.1 0.1 reshape.383
  97.3 0.1 compare_and_fusion
  97.4 1.2 gather_fusion.4
  98.6 1.2 gather_fusion.5
  99.9 0.6 iota_compare_fusion.5
  100.4 0.1 fusion.37
  100.5 0.7 fusion.45
  101.2 5.0 %fusion.32 = pred[64]{0:T(512)(128)(4,1)S(1)} fusion(s32[]{:T(128)} %bitcast.20, s32[]{:T(128)} %bitcast.21, s32[]{:T(128)} %bitcast.22, s32[]{:T(128)} %bitcast.23, s32[]{:T(128)} %bitcast.24, s32[]{:T(128)} %bitcast.26, s32[]{:T(128)} %bitcast.25, s32[]{:T(128)} %bitcast.19), kind=kLoop, calls=%fused_computation.91 | loop fusion | flops 2880 | bytes 96 | tf_op jit(solution)/shard_map/lt | solution.py:82
  106.2 0.1 select_add_fusion
  106.3 0.1 add_and_fusion
  106.4 35.1 %all-gather.9.cloned.1.call-done = bf16[16,8,256,256]{3,2,1,0:T(8,128)(2,1)} async-done(((bf16[1,8,256,256]{3,2,1,0:T(8,128)(2,1)}), bf16[16,8,256,256]{3,2,1,0:T(8,128)(2,1)}) %all-gather.9.cloned.1.call-update) | async-done | bytes 16777232 | tf_op jit(solution)/shard_map/all_gather | solution.py:44
  141.5 11.8 %gather_fusion.3 = bf16[72,256,256]{2,1,0:T(8,128)(2,1)} fusion(bf16[128,256,256]{2,1,0:T(8,128)(2,1)} %bitcast.96, s32[1024]{0:T(1024)S(1)} %pad_clamp_fusion), kind=kCustom, calls=%fused_computation.5 | custom fusion | bytes 18874656 | tf_op jit(solution)/shard_map/jit(_take)/gather | solution.py:89
  153.3 13.3 %all-gather.11.cloned.1.call-done = bf16[2048,256]{1,0:T(8,128)(2,1)} async-done(((bf16[256,256]{1,0:T(8,128)(2,1)}), bf16[2048,256]{1,0:T(8,128)(2,1)}) %all-gather.11.cloned.1.call-update) | async-done | bytes 1048592 | tf_op jit(solution)/shard_map/all_gather | solution.py:26
  166.6 51.8 %all-gather.7.cloned.1.call-done = bf16[1,64,256,256]{3,2,0,1:T(8,128)(2,1)} async-done(((bf16[1,8,256,256]{3,2,0,1:T(8,128)(2,1)}), bf16[1,64,256,256]{3,2,0,1:T(8,128)(2,1)}) %all-gather.7.cloned.1.call-update) | async-done | bytes 8388624 | tf_op jit(solution)/shard_map/all_gather | solution.py:51
  218.4 13.5 %fusion.2 = f32[72,256,256]{2,1,0:T(8,128)} fusion(bf16[8,256,256]{2,1,0:T(8,128)(2,1)} %bitcast.105, bf16[64,256,256]{2,1,0:T(8,128)(2,1)} %bitcast.104, bf16[72,256,256]{2,1,0:T(8,128)(2,1)} %gather_fusion.3, pred[72]{0:T(512)(128)(4,1)S(1)} %get-tuple-element.16), kind=kOutput, calls=%fused_computation.8 | convolution fusion | flops 2425356288 | bytes 37748808 | tf_op jit(solution)/shard_map/axy,ayz->axz/dot_general | solution.py:94
  231.9 0.0 copy-start.1
  231.9 24.1 %fusion = f32[32,256,256]{2,0,1:T(8,128)S(1)} fusion(f32[72,256,256]{2,1,0:T(8,128)} %fusion.2, s32[72]{0:T(128)S(1)} %select_add_fusion, pred[72]{0:T(512)(128)(4,1)S(1)} %add_and_fusion), kind=kOutput, calls=%fused_computation.6 | convolution fusion | flops 1811943936 | bytes 27263336 | tf_op jit(solution)/shard_map/ap,axz->pxz/dot_general | solution.py:96
  256.0 0.0 copy-done.1
  256.0 5.2 %subtract_reduce_fusion = (f32[]{:T(128)}, bf16[32,256,256]{2,0,1:T(8,128)(2,1)}) fusion(f32[32,256,256]{2,0,1:T(8,128)S(1)} %fusion, bf16[16,256,256]{2,1,0:T(8,128)(2,1)S(1)} %bitcast.95, s32[16]{0:T(128)S(1)} %bitcast.101, pred[16]{0:T(512)(128)(4,1)S(1)} %iota_compare_fusion.6), kind=kOutput, calls=%fused_computation.14 | convolution fusion | flops 77595648 | bytes 14680148 | tf_op jit(solution)/shard_map/sp,sxz->pxz/dot_general | solution.py:99
  261.2 9.0 %psum.28 = f32[]{:T(128)} all-reduce(f32[]{:T(128)} %get-tuple-element.18), channel_id=1, replica_groups=mesh['row_0'=4,'row_1'=4,'col_0'=4,'col_1'=2] {'row_0'}, use_global_device_ids=true, to_apply=%region_5.7 | all-reduce | flops 1 | bytes 8 | tf_op jit(solution)/shard_map/psum | solution.py:32
  270.3 9.0 %psum.29 = f32[]{:T(128)} all-reduce(f32[]{:T(128)} %psum.28), channel_id=1, replica_groups=mesh['row_0'=4,'row_1'=4,'col_0'=4,'col_1'=2] {'row_1'}, use_global_device_ids=true, to_apply=%region_6.8 | all-reduce | flops 1 | bytes 8 | tf_op jit(solution)/shard_map/psum | solution.py:32
  279.3 7.1 %psum.30 = f32[]{:T(128)} all-reduce(f32[]{:T(128)} %psum.29), channel_id=1, replica_groups=mesh['row_0'=4,'row_1'=4,'col_0'=4,'col_1'=2] {'col_0'}, use_global_device_ids=true, to_apply=%region_7.9 | all-reduce | flops 1 | bytes 8 | tf_op jit(solution)/shard_map/psum | solution.py:32
  286.4 9.3 %psum.31 = f32[]{:T(128)} all-reduce(f32[]{:T(128)} %psum.30), channel_id=1, replica_groups=mesh['row_0'=4,'row_1'=4,'col_0'=4,'col_1'=2] {'col_1'}, use_global_device_ids=true, to_apply=%region_8.10 | all-reduce | flops 1 | bytes 8 | tf_op jit(solution)/shard_map/psum | solution.py:32
  295.6 2.5 copy.26
  298.1 4.2 %copy.28 = bf16[64,8,16,256]{3,1,2,0:T(8,128)(2,1)} copy(bf16[64,8,16,256]{3,2,1,0:T(8,128)(2,1)S(1)} %bitcast.93) | data formatting | bytes 8388608
  (19 shorter events, 0.1 us)
Async XLA Ops:
  8.0 49.4 %copy-start = (bf16[1,16,256,256]{3,2,1,0:T(8,128)(2,1)S(1)}, bf16[1,16,256,256]{3,2,1,0:T(8,128)(2,1)}, u32[]{:S(2)}) copy-start(bf16[1,16,256,256]{3,2,1,0:T(8,128)(2,1)} %param.8) | copy-start | bytes 6291460
  8.0 52.7 %copy-start.2 = (s32[1,8]{1,0:T(1,128)S(1)}, s32[1,8]{1,0:T(1,128)}, u32[]{:S(2)}) copy-start(s32[1,8]{1,0:T(1,128)} %param.12) | copy-start | bytes 100
  8.0 71.2 %copy-start.3 = (s32[1,8]{1,0:T(1,128)S(1)}, s32[1,8]{1,0:T(1,128)}, u32[]{:S(2)}) copy-start(s32[1,8]{1,0:T(1,128)} %param.13) | copy-start | bytes 100
  8.0 49.3 %reduce-scatter.2.cloned.1.call-start = ((), (), s32[]{:S(2)}) async-start(), calls=%async_computation.2 | async-start | bytes 1179648 | tf_op jit(solution)/shard_map/reduce_scatter | solution.py:23
  27.3 114.2 %all-gather.9.cloned.1.call-start = ((), (), s32[]{:S(2)}) async-start(), calls=%async_computation.3 | async-start | bytes 17825792 | tf_op jit(solution)/shard_map/all_gather | solution.py:44
  27.8 138.7 %all-gather.11.cloned.1.call-start = ((), (), s32[]{:S(2)}) async-start(), calls=%async_computation.4 | async-start | bytes 1179648 | tf_op jit(solution)/shard_map/all_gather | solution.py:26
  57.3 161.1 %all-gather.7.cloned.1.call-start = ((), (), s32[]{:S(2)}) async-start(), calls=%async_computation.1 | async-start | bytes 9437184 | tf_op jit(solution)/shard_map/all_gather | solution.py:51
  231.9 24.1 %copy-start.1 = (s32[1,16]{1,0:T(1,128)S(1)}, s32[1,16]{1,0:T(1,128)}, u32[]{:S(2)}) copy-start(s32[1,16]{1,0:T(1,128)} %param.9) | copy-start | bytes 196
Sparse Core Ops, SparseCore 0:
  27.4 29.8 reduce-scatter.1
Sparse Core Ops, SparseCore 1:
  29.9 111.5 all-gather.8
  143.1 23.5 all-gather.10
  168.8 49.6 all-gather.6
where the time goes:
time: 312 us
  waiting for transfers between devices  130 us (42%)
  blocking collectives  78.7 us (25%)
  matrix products  43.4 us (14%)
  local copies, waits for them, and re-layouts  31.2 us (10%)
  between operations  19.8 us (6%)
  other arithmetic  8.28 us (3%)
    all_gather x1, waiting for transfers between devices, on_device(): lax.all_gather(band_tiles[:, :half], COL, axis=1, tiled=True)  51.8 us
    all_gather x1, waiting for transfers between devices, on_device(): lax.all_gather(matrix_tiles, ROW, axis=0, tiled=True)  35.1 us
    psum x4, blocking collectives, over_axes(): shard = lax.psum(shard, axis)  34.4 us
    reduce_scatter x1, waiting for transfers between devices, sum_by_parts(): lax.psum_scatter(rows_for(lines, lax.axis_size(axis)), axis, scatter_dime...  29.4 us
    dot_general x1, matrix products, on_device(): jnp.einsum('ap,axz->pxz', weights, product, precision=lax.Precision.HIGHEST)  24.1 us
    all_gather x1, blocking collectives, on_device(): lax.all_gather(matrix_live, ROW, axis=0, tiled=True)  17.3 us
    all_gather x1, blocking collectives, on_device(): lax.all_gather(matrix_col, ROW, axis=0, tiled=True)  17.2 us
    dot_general x1, matrix products, on_device(): jnp.einsum('axy,ayz->axz', tiles, picked, preferred_element_type=jnp.floa...  13.5 us
  transfers between devices with their start and end apart: 4, of which 4 were waited for; matrix products, arithmetic and copies ran while one was open for 8% of the time, Pallas kernels for 0%

commit v1 on v0

--- a/solution.py
+++ b/solution.py
@@ -41,7 +41,9 @@
     places = BR * tcols
     spots = jnp.arange(places, dtype=jnp.int32)
     b_tiles, b_index, b_live = (
-        lax.all_gather(matrix_tiles, ROW, axis=0, tiled=True),
+        jnp.concatenate(
+            lax.all_to_all(jnp.stack([matrix_tiles] * lax.axis_size(ROW)), ROW, 0, 0), axis=0
+        ),
         lax.all_gather(matrix_col, ROW, axis=0, tiled=True),
         lax.all_gather(matrix_live, ROW, axis=0, tiled=True),
     )

time: 312 us -> 474 us (1.52)
  blocking collectives: 78.7 us -> 324 us
  waiting for transfers between devices: 130 us -> 29.7 us
  local copies, waits for them, and re-layouts: 31.2 us -> 42.1 us
  starting transfers between devices: 0.16 us -> 6.96 us
    all_gather x1, blocking collectives: 17.2 us -> 247 us  [on_device(): lax.all_gather(matrix_col, ROW, axis=0, tiled=True)]
    all_gather x1, waiting for transfers between devices: 51.8 us -> 0.01 us  [on_device(): lax.all_gather(band_tiles[:, :half], COL, axis=1, tiled=True)]
    all_gather x1 -> x0, waiting for transfers between devices: 35.1 us -> none  [on_device(): lax.all_gather(matrix_tiles, ROW, axis=0, tiled=True)]
    psum x4, blocking collectives: 34.4 us -> 54.5 us  [over_axes(): shard = lax.psum(shard, axis)]
    all_gather x1, waiting for transfers between devices: 13.3 us -> 0.01 us  [sum_by_parts(): whole = lax.all_gather(own, axis).reshape(-1, *lines.shape[1:])]
    all_to_all x0 -> x1, starting transfers between devices: none -> 6.84 us  [on_device(): lax.all_to_all(jnp.stack([matrix_tiles] * lax.axis_size(ROW)), ROW, 0, 0)]
    another operation x0 -> x1, local copies, waits for them, and re-layouts: none -> 6.81 us  [on_device(): jnp.stack([matrix_tiles] * lax.axis_size(ROW))]
  transfers between devices with their start and end apart: 4 -> 4, of which waited for: 4 -> 1; matrix products, arithmetic and copies ran while one was open for 8% -> 7% of each run, Pallas kernels for 0% -> 0%
where the time goes in v1:
time: 474 us; the launch traced here: 473 us
  blocking collectives  324 us (68%)
  matrix products  43.5 us (9%)
  local copies, waits for them, and re-layouts  42.1 us (9%)
  waiting for transfers between devices  29.7 us (6%)
  between operations  17.7 us (4%)
  other arithmetic  8.48 us (2%)
  starting transfers between devices  6.96 us (1%)
    all_gather x1, blocking collectives, on_device(): lax.all_gather(matrix_col, ROW, axis=0, tiled=True)  247 us
    psum x4, blocking collectives, over_axes(): shard = lax.psum(shard, axis)  54.5 us
    reduce_scatter x1, waiting for transfers between devices, sum_by_parts(): lax.psum_scatter(rows_for(lines, lax.axis_size(axis)), axis, scatter_dime...  29.7 us
    dot_general x1, matrix products, on_device(): jnp.einsum('ap,axz->pxz', weights, product, precision=lax.Precision.HIGHEST)  24.1 us
    all_gather x1, blocking collectives, on_device(): lax.all_gather(matrix_live, ROW, axis=0, tiled=True)  13.6 us
    dot_general x1, matrix products, on_device(): jnp.einsum('axy,ayz->axz', tiles, picked, preferred_element_type=jnp.floa...  13.5 us
    gather x1, local copies, waits for them, and re-layouts, on_device(): picked = jnp.take(flat_tiles, k_glob, axis=0)  11.8 us
    unnamed x1, blocking collectives  9.78 us
  transfers between devices with their start and end apart: 4, of which 1 were waited for; matrix products, arithmetic and copies ran while one was open for 7% of the time, Pallas kernels for 0%

profile of v1, /device:TPU:1, one launch (start us, length us, event | category | flops | bytes accessed | tf_op | source)
XLA Modules:
  0.0 472.9 jit_solution(10398335396985986402)
XLA Ops:
  7.2 0.0 reduce-scatter.2.cloned.1.call-start
  7.9 1.2 dynamic-slice.3
  9.8 0.7 bitcast_dynamic-update-slice_fusion
  10.5 0.8 bitcast_dynamic-update-slice_fusion.1
  11.2 9.8 %all-reduce.2 = (s32[8]{0:T(128)S(1)}, s32[128]{0:T(128)S(1)}) all-reduce(s32[8]{0:T(128)S(1)} %bitcast_dynamic-update-slice_fusion, s32[128]{0:T(128)S(1)} %bitcast_dynamic-update-slice_fusion.1), channel_id=1, replica_groups=mesh['row_0'=4,'row_1'=4,'col_0'=4,'col_1'=2] {'col_0','col_1'}, use_global_device_ids=true, to_apply=%add.1 | all-reduce | flops 136 | bytes 1088
  21.0 0.7 fusion.42
  21.7 0.2 reduce-window.8
  21.9 0.6 dynamic-slice.2
  23.1 1.3 slice.7
  24.4 0.7 convolution_convert_fusion
  25.1 1.2 copy.24
  26.3 0.0 reduce-scatter.2.cloned.1.call-update
  26.3 0.0 all-gather.8.cloned.1.call-start
  26.4 29.7 %reduce-scatter.2.cloned.1.call-done = bf16[256,256]{1,0:T(8,128)(2,1)} async-done(((bf16[2048,256]{1,0:T(8,128)(2,1)}), bf16[256,256]{1,0:T(8,128)(2,1)}) %reduce-scatter.2.cloned.1.call-update) | async-done | bytes 131088 | tf_op jit(solution)/shard_map/reduce_scatter | solution.py:23
  56.1 0.0 all-gather.8.cloned.1.call-update
  56.1 6.8 %stack.2 = bf16[16,1,8,256,256]{4,3,2,1,0:T(8,128)(2,1)} broadcast(bf16[8,256,256]{2,1,0:T(8,128)(2,1)} %bitcast.99), dimensions={2,3,4} | broadcast | bytes 17825792 | tf_op jit(solution)/shard_map/stack | solution.py:45
  62.9 0.0 copy-start
  62.9 0.0 copy-start.2
  62.9 0.0 copy-start.3
  62.9 6.8 %all-to-all-start = ((bf16[16,1,8,256,256]{4,3,2,1,0:T(8,128)(2,1)}), bf16[16,1,8,256,256]{4,3,2,1,0:T(8,128)(2,1)}, u32[]{:S(2)}, u32[]{:S(2)}) async-start(bf16[16,1,8,256,256]{4,3,2,1,0:T(8,128)(2,1)} %stack.2), calls=%async_computation.1 | async-start | bytes 33554432 | tf_op jit(solution)/shard_map/all_to_all | solution.py:45
  69.8 0.0 all-gather.6.cloned.1.call-start
  69.8 0.0 copy-done
  69.8 1.0 slice.43
  70.9 0.0 all-gather.6.cloned.1.call-update
  70.9 0.1 convert_reduce_fusion
  71.0 0.6 gather_fusion.1
  71.7 0.6 gather_fusion.2
  72.4 0.8 gather_fusion
  73.2 0.0 copy-done.2
  73.2 246.5 %all-gather.1 = s32[16,1,8]{2,1,0:T(1,128)S(1)} all-gather(s32[1,1,8]{2,1,0:T(1,128)S(1)} %bitcast.103), channel_id=1, replica_groups=mesh['row_0'=4,'row_1'=4,'col_0'=4,'col_1'=2] {'row_0','row_1'}, dimensions={0}, use_global_device_ids=true | all-gather | bytes 544 | tf_op jit(solution)/shard_map/all_gather | solution.py:47
  319.7 0.5 broadcast.1068
  320.2 0.7 reduce.7
  320.8 0.1 reshape.382
  320.9 0.0 copy-done.3
  320.9 13.6 %all-gather.2 = s32[16,1,8]{2,1,0:T(1,128)S(1)} all-gather(s32[1,1,8]{2,1,0:T(1,128)S(1)} %bitcast.104), channel_id=1, replica_groups=mesh['row_0'=4,'row_1'=4,'col_0'=4,'col_1'=2] {'row_0','row_1'}, dimensions={0}, use_global_device_ids=true | all-gather | bytes 544 | tf_op jit(solution)/shard_map/all_gather | solution.py:48
  334.5 0.7 reduce.8
  335.2 0.1 reshape.383
  335.3 0.1 compare_and_fusion
  335.4 1.2 gather_fusion.4
  336.6 1.2 gather_fusion.5
  337.9 0.6 iota_compare_fusion.5
  338.6 0.1 fusion.37
  338.6 0.7 fusion.45
  339.3 5.1 %fusion.32 = pred[64]{0:T(512)(128)(4,1)S(1)} fusion(s32[]{:T(128)} %bitcast.20, s32[]{:T(128)} %bitcast.21, s32[]{:T(128)} %bitcast.22, s32[]{:T(128)} %bitcast.23, s32[]{:T(128)} %bitcast.24, s32[]{:T(128)} %bitcast.26, s32[]{:T(128)} %bitcast.25, s32[]{:T(128)} %bitcast.19), kind=kLoop, calls=%fused_computation.91 | loop fusion | flops 2880 | bytes 96 | tf_op jit(solution)/shard_map/lt | solution.py:84
  344.4 0.1 select_add_fusion
  344.5 0.1 add_and_fusion
  344.6 0.0 all-to-all-done
  344.6 11.8 %gather_fusion.3 = bf16[72,256,256]{2,1,0:T(8,128)(2,1)} fusion(bf16[128,256,256]{2,1,0:T(8,128)(2,1)} %bitcast.38, s32[1024]{0:T(1024)S(1)} %pad_clamp_fusion), kind=kCustom, calls=%fused_computation.5 | custom fusion | bytes 18874656 | tf_op jit(solution)/shard_map/jit(_take)/gather | solution.py:91
  356.4 0.0 all-gather.8.cloned.1.call-done
  356.4 0.0 all-gather.6.cloned.1.call-done
  356.4 13.5 %fusion.2 = f32[72,256,256]{2,1,0:T(8,128)} fusion(bf16[8,256,256]{2,1,0:T(8,128)(2,1)} %bitcast.106, bf16[64,256,256]{2,1,0:T(8,128)(2,1)} %bitcast.105, bf16[72,256,256]{2,1,0:T(8,128)(2,1)} %gather_fusion.3, pred[72]{0:T(512)(128)(4,1)S(1)} %get-tuple-element.16), kind=kOutput, calls=%fused_computation.8 | convolution fusion | flops 2425356288 | bytes 37748808 | tf_op jit(solution)/shard_map/axy,ayz->axz/dot_general | solution.py:96
  369.9 0.0 copy-start.1
  369.9 24.1 %fusion = f32[32,256,256]{2,0,1:T(8,128)S(1)} fusion(f32[72,256,256]{2,1,0:T(8,128)} %fusion.2, s32[72]{0:T(128)S(1)} %select_add_fusion, pred[72]{0:T(512)(128)(4,1)S(1)} %add_and_fusion), kind=kOutput, calls=%fused_computation.6 | convolution fusion | flops 1811943936 | bytes 27263336 | tf_op jit(solution)/shard_map/ap,axz->pxz/dot_general | solution.py:98
  394.0 0.0 copy-done.1
  394.0 5.2 %subtract_reduce_fusion = (f32[]{:T(128)}, bf16[32,256,256]{2,0,1:T(8,128)(2,1)}) fusion(f32[32,256,256]{2,0,1:T(8,128)S(1)} %fusion, bf16[16,256,256]{2,1,0:T(8,128)(2,1)S(1)} %bitcast.96, s32[16]{0:T(128)S(1)} %bitcast.102, pred[16]{0:T(512)(128)(4,1)S(1)} %iota_compare_fusion.6), kind=kOutput, calls=%fused_computation.14 | convolution fusion | flops 77595648 | bytes 14680148 | tf_op jit(solution)/shard_map/sp,sxz->pxz/dot_general | solution.py:101
  399.2 8.0 %psum.28 = f32[]{:T(128)} all-reduce(f32[]{:T(128)} %get-tuple-element.18), channel_id=1, replica_groups=mesh['row_0'=4,'row_1'=4,'col_0'=4,'col_1'=2] {'row_0'}, use_global_device_ids=true, to_apply=%region_5.7 | all-reduce | flops 1 | bytes 8 | tf_op jit(solution)/shard_map/psum | solution.py:32
  407.3 6.9 %psum.29 = f32[]{:T(128)} all-reduce(f32[]{:T(128)} %psum.28), channel_id=1, replica_groups=mesh['row_0'=4,'row_1'=4,'col_0'=4,'col_1'=2] {'row_1'}, use_global_device_ids=true, to_apply=%region_6.8 | all-reduce | flops 1 | bytes 8 | tf_op jit(solution)/shard_map/psum | solution.py:32
  414.2 4.4 copy.26
  418.6 22.1 %psum.30 = f32[]{:T(128)} all-reduce(f32[]{:T(128)} %psum.29), channel_id=1, replica_groups=mesh['row_0'=4,'row_1'=4,'col_0'=4,'col_1'=2] {'col_0'}, use_global_device_ids=true, to_apply=%region_7.9 | all-reduce | flops 1 | bytes 8 | tf_op jit(solution)/shard_map/psum | solution.py:32
  440.7 6.4 %copy.28 = bf16[64,8,16,256]{3,1,2,0:T(8,128)(2,1)} copy(bf16[64,8,16,256]{3,2,1,0:T(8,128)(2,1)} %bitcast.94) | data formatting | bytes 8388608
  447.1 17.5 %psum.31 = f32[]{:T(128)} all-reduce(f32[]{:T(128)} %psum.30), channel_id=1, replica_groups=mesh['row_0'=4,'row_1'=4,'col_0'=4,'col_1'=2] {'col_1'}, use_global_device_ids=true, to_apply=%region_8.10 | all-reduce | flops 1 | bytes 8 | tf_op jit(solution)/shard_map/psum | solution.py:32
  (19 shorter events, 0.1 us)
Async XLA Ops:
  7.2 48.9 %reduce-scatter.2.cloned.1.call-start = ((), (), s32[]{:S(2)}) async-start(), calls=%async_computation.3 | async-start | bytes 1179648 | tf_op jit(solution)/shard_map/reduce_scatter | solution.py:23
  26.3 330.0 %all-gather.8.cloned.1.call-start = ((), (), s32[]{:S(2)}) async-start(), calls=%async_computation.4 | async-start | bytes 1179648 | tf_op jit(solution)/shard_map/all_gather | solution.py:26
  62.9 6.9 %copy-start = (bf16[1,16,256,256]{3,2,1,0:T(8,128)(2,1)S(1)}, bf16[1,16,256,256]{3,2,1,0:T(8,128)(2,1)}, u32[]{:S(2)}) copy-start(bf16[1,16,256,256]{3,2,1,0:T(8,128)(2,1)} %param.8) | copy-start | bytes 6291460
  62.9 10.3 %copy-start.2 = (s32[1,8]{1,0:T(1,128)S(1)}, s32[1,8]{1,0:T(1,128)}, u32[]{:S(2)}) copy-start(s32[1,8]{1,0:T(1,128)} %param.12) | copy-start | bytes 100
  62.9 258.0 %copy-start.3 = (s32[1,8]{1,0:T(1,128)S(1)}, s32[1,8]{1,0:T(1,128)}, u32[]{:S(2)}) copy-start(s32[1,8]{1,0:T(1,128)} %param.13) | copy-start | bytes 100
  62.9 281.6 %all-to-all-start = ((bf16[16,1,8,256,256]{4,3,2,1,0:T(8,128)(2,1)}), bf16[16,1,8,256,256]{4,3,2,1,0:T(8,128)(2,1)}, u32[]{:S(2)}, u32[]{:S(2)}) async-start(bf16[16,1,8,256,256]{4,3,2,1,0:T(8,128)(2,1)} %stack.2), calls=%async_computation.1 | async-start | bytes 33554432 | tf_op jit(solution)/shard_map/all_to_all | solution.py:45
  69.8 286.6 %all-gather.6.cloned.1.call-start = ((), (), s32[]{:S(2)}) async-start(), calls=%async_computation.2 | async-start | bytes 9437184 | tf_op jit(solution)/shard_map/all_gather | solution.py:53
  369.9 24.1 %copy-start.1 = (s32[1,16]{1,0:T(1,128)S(1)}, s32[1,16]{1,0:T(1,128)}, u32[]{:S(2)}) copy-start(s32[1,16]{1,0:T(1,128)} %param.9) | copy-start | bytes 196
Sparse Core Ops, SparseCore 0:
  26.5 29.5 reduce-scatter.1
  57.8 25.6 all-gather.7
  85.8 49.8 all-gather.5
